TPU v7x, 32 devices: a whole 2x2x4 slice. The times are simulated.
32 devices in a mesh: row: 8 (over z, x), col: 4 (over y, core).
Axes of the slice: x: 2, y: 2, z: 4, core: 2. Of those that a mesh axis runs over, the one named last changes fastest.
Arguments:
- front_base: float32 [16, 8, 128, 32, 4, 128], P(None, 'row', None, None, 'col')
- traces: bfloat16 [16, 8, 4, 3, 128, 128], P(None, 'row'), may hold values from -0.75 to 0.75
- adjacency: int32 [128, 4], replicated, may hold values from 0 to 127, as said below
- pivot_order: int32 [2, 512], replicated, may hold values from 0 to 511, each once within a row
- pivot_kind: int32 [2, 512], replicated, may hold values from 0 to 2, as said below
- inverse_diagonal: float32 [2, 512], replicated, may hold values from -0.3 to 0.3
- inverse_coupling: float32 [2, 512], replicated, may hold values from -0.3 to 0.3
- readers: int32 [2, 128], replicated, may hold values 0 or 1
Outputs:
- trailing: float32 [16, 8, 128, 32, 4, 128], P(None, 'row', None, None, 'col')
Inputs may be any that keep to these rules, and one draw needn't show every extreme that they name: The elements form a 16 x 8 grid that closes on itself in both dimensions, numbered in a drawn order; faces 0 and 1 lead to the next and previous element along the first dimension, 2 and 3 along the second, so adjacency[adjacency[e, f], f with its lowest bit flipped] = e. `pivot_kind`: 0 marks a 1 x 1 pivot; 1 marks the first position of a 2 x 2 pivot, whose second position follows and is marked 2; 2 x 2 pivots start at even positions.
All inputs are finite; a program needn't handle non-finite values.
Results may differ from a plain program's by a relative error of at most 0.008.
Values may be sent and summed in bfloat16 or wider, within the bound.
A program may use at most 256 MiB of HBM per device.

v0:
```python
import jax
import jax.numpy as jnp
from jax import lax
from jax.sharding import PartitionSpec as P

NB = 128
PW = 512
PANELS = 2


def from_root(array, axis, root):
    mine = lax.axis_index(axis) == root
    return lax.psum(jnp.where(mine, array, jnp.zeros_like(array)), axis)


def face_left(values):
    return jnp.concatenate(
        [values[:, :, 0], values[:, :, 0], values[:, :, 1], values[:, :, 2]], axis=2
    )


def face_right(values):
    return jnp.concatenate(
        [
            4.0 * values[:, :, 0],
            -0.5 * values[:, :, 1],
            -0.5 * values[:, :, 0],
            2.0 * values[:, :, 2],
        ],
        axis=2,
    )


def apply_inverse(values, pivot_kinds, diagonal, pair_terms):
    starts = (pivot_kinds == 1).astype(values.dtype)
    upward = pair_terms * starts
    upward_prev = jnp.concatenate([jnp.zeros_like(upward[:1]), upward[:-1]])
    following = jnp.concatenate([values[:, 1:], jnp.zeros_like(values[:, :1])], axis=1)
    preceding = jnp.concatenate([jnp.zeros_like(values[:, :1]), values[:, :-1]], axis=1)
    return values * diagonal + following * upward + preceding * upward_prev


def local(
    front_base,
    traces,
    adjacency,
    pivot_order,
    pivot_kind,
    inverse_diagonal,
    inverse_coupling,
    readers,
):
    row_count = lax.axis_size("row")
    col_count = lax.axis_size("col")
    row_index = lax.axis_index("row")
    col_index = lax.axis_index("col")
    row_blocks = front_base.shape[0]
    col_blocks = front_base.shape[3]
    row_groups = row_count // col_count
    rows_total = row_blocks * NB
    local_traces = traces[:, 0]
    received = []
    for copy_index in range(row_groups):
        received.append(from_root(local_traces, "row", col_index + copy_index * col_count))
    column_traces = jnp.stack(received, axis=1).reshape((col_blocks,) + local_traces.shape[1:])
    left_parts = face_left(local_traces)
    right_parts = face_right(local_traces)
    column_right = face_right(column_traces)
    opposite = jnp.array([1, 0, 3, 2], dtype=jnp.int32)
    local_elements = jnp.arange(row_blocks, dtype=jnp.int32) * row_count + row_index
    neighbour = jnp.take(adjacency, local_elements, axis=0)
    held_here = neighbour % col_count == col_index
    col_slot = neighbour // col_count
    partner = column_right[col_slot, opposite[None, :]]
    coupling = jnp.einsum(
        "efqi,efqj->efij", left_parts, partner, preferred_element_type=jnp.float32
    )
    self_terms = jnp.einsum(
        "efqi,efqj->eij", left_parts, right_parts, preferred_element_type=jnp.float32
    )
    slot_ids = jnp.arange(col_blocks, dtype=jnp.int32)
    place_pair = (held_here[:, :, None] & (col_slot[:, :, None] == slot_ids[None, None, :])).astype(
        jnp.float32
    )
    self_here = (local_elements % col_count == col_index)[:, None]
    place_self = (self_here & ((local_elements // col_count)[:, None] == slot_ids[None, :])).astype(
        jnp.float32
    )
    assembled = jnp.einsum("eij,ec->eicj", self_terms, place_self, precision=lax.Precision.HIGHEST)
    assembled = assembled - jnp.einsum(
        "efij,efc->eicj", coupling, place_pair, precision=lax.Precision.HIGHEST
    )
    front_mat = front_base.reshape(rows_total, col_blocks * NB) + assembled.reshape(
        rows_total, col_blocks * NB
    )
    panel_blocks = PW // NB
    for which_panel in range(PANELS):
        first_block = which_panel * panel_blocks
        front_slots = front_mat.reshape(rows_total, col_blocks, NB)
        low_slot = first_block // col_count
        high_slot = (first_block + panel_blocks - 1) // col_count
        slab_cols = front_slots[:, low_slot : high_slot + 1, :].astype(jnp.bfloat16)[:, :, None, :]
        gathered = lax.all_gather(slab_cols, "col", axis=2, tiled=True)
        gathered = gathered.reshape(rows_total, -1, NB)
        begin_block = first_block - low_slot * col_count
        columns = gathered[:, begin_block : begin_block + panel_blocks, :].reshape(rows_total, PW)
        columns = jnp.take(columns, pivot_order[which_panel], axis=1)
        kept_blocks = jnp.take(readers[which_panel], local_elements) * (
            local_elements >= first_block + panel_blocks
        ).astype(jnp.int32)
        kept_rows = jnp.repeat(kept_blocks, NB).astype(jnp.bfloat16)
        panel_vals = columns * kept_rows[:, None]
        scaled = apply_inverse(
            panel_vals.astype(jnp.float32),
            pivot_kind[which_panel],
            inverse_diagonal[which_panel],
            inverse_coupling[which_panel],
        ).astype(jnp.bfloat16)
        transposed = []
        for copy_index in range(row_groups):
            incoming = from_root(panel_vals, "row", col_index + copy_index * col_count)
            transposed.append(incoming.reshape(row_blocks, NB, PW))
        col_panel = jnp.stack(transposed, axis=1).reshape(col_blocks * NB, PW)
        front_mat = front_mat - lax.dot_general(
            scaled, col_panel, (((1,), (1,)), ((), ())), preferred_element_type=jnp.float32
        )
    return front_mat.reshape(row_blocks, 1, NB, col_blocks, 1, NB)


def solution(mesh):
    in_specs = (
        P(None, "row", None, None, "col", None),
        P(None, "row", None, None, None, None),
        P(),
        P(),
        P(),
        P(),
        P(),
        P(),
    )
    out_specs = P(None, "row", None, None, "col", None)
    return jax.shard_map(local, mesh=mesh, in_specs=in_specs, out_specs=out_specs, check_vma=False)
```

profile of v0, /device:TPU:0, one launch (start us, length us, event | category | flops | bytes accessed | tf_op | source)
XLA Modules:
  0.0 1033.8 jit_solution(11195082344571831130)
XLA Ops:
  6.5 7.4 select_bitcast_fusion.1
  14.1 8.1 copy.85
  23.3 26.3 %copy.45 = f32[16,1,128,32,1,128]{5,2,0,3,4,1:T(8,128)} copy(f32[16,1,128,32,1,128]{5,4,3,2,1,0:T(1,128)} %param.13) | data formatting | bytes 67108864 | tf_op args[0]
  56.0 8.4 fusion.20
  64.4 350.9 %all-reduce.15.cloned.1.call-done = (bf16[16,1,4,3,128,128]{5,4,2,0,3,1:T(8,128)(2,1)}, bf16[16,1,4,3,128,128]{5,4,2,0,3,1:T(8,128)(2,1)}) async-done(((bf16[16,1,4,3,128,128]{5,4,2,0,3,1:T(8,128)(2,1)}, bf16[16,1,4,3,128,128]{5,4,2,0,3,1:T(8,128)(2,1)}), (bf16[16,1,4,3,128,128]{5,4,2,0,3,1:T(8,128)(2,1)}, bf16[16,1,4,3,128,128]{5,4,2,0,3,1:T(8,128)(2,1)})) %all-reduce.15.cloned.1.call-update) | async-done | bytes 12582928 | tf_op jit(solution)/shard_map/psum | solution.py:13
  415.3 6.1 pad_maximum_fusion.1
  424.5 6.6 pad_maximum_fusion
  431.1 11.7 %gather_fusion.1 = bf16[64,512,128]{2,1,0:T(8,128)(2,1)} fusion(bf16[32,4,512,128]{3,2,1,0:T(8,128)(2,1)} %pad_maximum_fusion, s32[64]{0:T(128)S(1)} %reshape.307), kind=kCustom, calls=%fused_computation.5 | custom fusion | bytes 16777728 | tf_op jit(solution)/shard_map/gather | solution.py:74
  442.9 11.5 %fusion.13 = f32[16,4,128,128]{3,2,1,0:T(8,128)} fusion(bf16[16,4,512,128]{3,2,1,0:T(8,128)(2,1)} %bitcast.162, bf16[16,4,128,128]{3,2,1,0:T(8,128)(2,1)} %get-tuple-element.19, bf16[16,4,128,128]{3,2,1,0:T(8,128)(2,1)} %get-tuple-element.20, bf16[16,4,128,128]{3,2,1,0:T(8,128)(2,1)S(1)} %copy-done.3), kind=kOutput, calls=%fused_computation.38 | convolution fusion | flops 1107296256 | bytes 18874368 | tf_op jit(solution)/shard_map/efqi,efqj->efij/dot_general | solution.py:75
  454.4 24.8 %multiply_subtract_fusion = f32[16,32,128,128]{3,1,2,0:T(8,128)S(1)} fusion(f32[16,128,128]{2,1,0:T(8,128)} %fusion.20, f32[16,32]{1,0:T(8,128)S(1)} %fusion.33, f32[16,4,128,128]{3,2,1,0:T(8,128)} %fusion.13, s32[16,4]{1,0:T(8,128)S(1)} %add_select_fusion, pred[16,4]{1,0:T(8,128)(4,1)S(1)} %fusion.31), kind=kOutput, calls=%fused_computation.9 | convolution fusion | flops 419434496 | bytes 38799680 | tf_op jit(solution)/shard_map/efij,efc->eicj/dot_general | solution.py:90
  479.2 11.7 %copy-done = f32[16,32,128,128]{3,1,2,0:T(8,128)} copy-done((f32[16,32,128,128]{3,1,2,0:T(8,128)}, f32[16,32,128,128]{3,1,2,0:T(8,128)S(1)}, u32[]{:S(2)}) %copy-start) | copy-done | bytes 33554456
  495.1 21.0 %all-gather.5.cloned.1.call-done = bf16[2048,4,128]{2,0,1:T(8,128)(2,1)} async-done(((bf16[2048,1,128]{2,0,1:T(8,128)(2,1)}), bf16[2048,4,128]{2,0,1:T(8,128)(2,1)}) %all-gather.5.cloned.1.call-update) | async-done | bytes 2097168 | tf_op jit(solution)/shard_map/all_gather | solution.py:103
  522.4 4.9 fusion.49
  540.9 149.7 %all-reduce.13.cloned.1.call-done = (bf16[16,1,128,512]{3,2,1,0:T(8,128)(2,1)}, bf16[16,1,128,512]{3,2,1,0:T(8,128)(2,1)}) async-done(((bf16[16,1,128,512]{3,2,1,0:T(8,128)(2,1)}, bf16[16,1,128,512]{3,2,1,0:T(8,128)(2,1)}), (bf16[16,1,128,512]{3,2,1,0:T(8,128)(2,1)}, bf16[16,1,128,512]{3,2,1,0:T(8,128)(2,1)})) %all-reduce.13.cloned.1.call-update) | async-done | bytes 4194320 | tf_op jit(solution)/shard_map/psum | solution.py:13
  690.6 4.7 pad_maximum_fusion.3
  695.3 52.3 %fusion = f32[2048,4096]{1,0:T(8,128)} fusion(f32[256,8,32,128]{3,2,1,0:T(8,128)} %bitcast.150, f32[256,8,32,128]{3,2,1,0:T(8,128)} %bitcast.151, bf16[4096,512]{1,0:T(8,128)(2,1)} %bitcast.161, bf16[2048,512]{0,1:T(8,128)(2,1)S(1)} %add_convert_fusion.6), kind=kOutput, calls=%fused_computation.7 | convolution fusion | flops 8606711808 | bytes 106954752 | tf_op jit(solution)/shard_map/dot_general | solution.py:124
  747.5 12.1 %convert_bitcast_fusion = bf16[256,8,32,128]{3,1,2,0:T(8,128)(2,1)S(1)} fusion(f32[2048,4096]{1,0:T(8,128)} %fusion), kind=kLoop, calls=%fused_computation.11 | loop fusion | flops 8388608 | bytes 50331648
  766.2 20.9 %all-gather.7.cloned.1.call-done = bf16[2048,4,128]{2,0,1:T(8,128)(2,1)} async-done(((bf16[2048,1,128]{2,0,1:T(8,128)(2,1)}), bf16[2048,4,128]{2,0,1:T(8,128)(2,1)}) %all-gather.7.cloned.1.call-update) | async-done | bytes 2097168 | tf_op jit(solution)/shard_map/all_gather | solution.py:103
  793.4 4.9 fusion.50
  804.7 8.5 fusion.51
  813.2 148.3 %all-reduce.11.cloned.1.call-done = (bf16[16,1,128,512]{3,2,1,0:T(8,128)(2,1)}, bf16[16,1,128,512]{3,2,1,0:T(8,128)(2,1)}) async-done(((bf16[16,1,128,512]{3,2,1,0:T(8,128)(2,1)}, bf16[16,1,128,512]{3,2,1,0:T(8,128)(2,1)}), (bf16[16,1,128,512]{3,2,1,0:T(8,128)(2,1)}, bf16[16,1,128,512]{3,2,1,0:T(8,128)(2,1)})) %all-reduce.11.cloned.1.call-update) | async-done | bytes 4194320 | tf_op jit(solution)/shard_map/psum | solution.py:13
  961.5 4.8 pad_maximum_fusion.4
  966.3 32.9 %subtract_bitcast_fusion = f32[256,8,32,128]{3,1,2,0:T(8,128)} fusion(f32[2048,4096]{1,0:T(8,128)} %fusion, bf16[4096,512]{1,0:T(8,128)(2,1)} %bitcast.160, f32[2048,511]{0,1:T(8,128)} %get-tuple-element.26, f32[2048,511]{0,1:T(8,128)} %get-tuple-element.25, f32[512]{0:T(512)S(1)} %get-tuple-element.47, f32[512]{0:T(512)S(1)} %bitcast.168, ...), kind=kOutput, calls=%fused_computation.8 | convolution fusion | flops 8607760384 | bytes 81783296 | tf_op jit(solution)/shard_map/dot_general | solution.py:124
  999.2 27.6 %copy.70 = f32[256,8,32,128]{3,2,1,0:T(8,128)} copy(f32[256,8,32,128]{3,1,2,0:T(8,128)} %subtract_bitcast_fusion) | data formatting | bytes 67108864
  (87 shorter events, 53.6 us)
Async XLA Ops:
  6.5 408.7 %all-reduce.15.cloned.1.call-start = ((), (), s32[]{:S(2)}) async-start(), calls=%async_computation.4 | async-start | bytes 25165824 | tf_op jit(solution)/shard_map/psum | solution.py:13
  14.0 8.2 copy-start.8
  14.0 9.0 copy-start.10
  14.0 502.1 %all-gather.5.cloned.1.call-start = ((), (), s32[]{:S(2)}) async-start(), calls=%async_computation | async-start | bytes 2621440 | tf_op jit(solution)/shard_map/all_gather | solution.py:103
  23.2 26.7 %slice-start = ((s8[6291456]{0:T(1024)(128)(4,1)}), s8[2097152]{0:T(1024)(128)(4,1)S(1)}, s32[]{:S(2)}) async-start(s8[6291456]{0:T(1024)(128)(4,1)} %bitcast.152), calls=%async_computation.5 | async-start | bytes 4194304
  23.3 26.6 %slice-start.1 = ((s8[6291456]{0:T(1024)(128)(4,1)}), s8[4194304]{0:T(1024)(128)(4,1)S(1)}, s32[]{:S(2)}) async-start(s8[6291456]{0:T(1024)(128)(4,1)} %bitcast.152), calls=%async_computation.6 | async-start | bytes 8388608
  431.1 11.8 %copy-start.3 = (bf16[16,4,128,128]{3,2,1,0:T(8,128)(2,1)S(1)}, bf16[16,4,128,128]{3,2,1,0:T(8,128)(2,1)}, u32[]{:S(2)}) copy-start(bf16[16,4,128,128]{3,2,1,0:T(8,128)(2,1)} %get-tuple-element.18) | copy-start | bytes 6291460
  479.2 11.7 %copy-start = (f32[16,32,128,128]{3,1,2,0:T(8,128)}, f32[16,32,128,128]{3,1,2,0:T(8,128)S(1)}, u32[]{:S(2)}) copy-start(f32[16,32,128,128]{3,1,2,0:T(8,128)S(1)} %multiply_subtract_fusion) | copy-start | bytes 100663296
  479.2 15.1 %copy-start.9 = (s32[2,128]{1,0:T(2,128)S(1)}, s32[2,128]{1,0:T(2,128)}, u32[]{:S(2)}) copy-start(s32[2,128]{1,0:T(2,128)} %param.20) | copy-start | bytes 3076
  479.2 15.8 %copy-start.6 = (s32[2,512]{1,0:T(2,128)S(1)}, s32[2,512]{1,0:T(2,128)}, u32[]{:S(2)}) copy-start(s32[2,512]{1,0:T(2,128)} %param.16) | copy-start | bytes 12292
  494.2 196.4 %all-reduce.13.cloned.1.call-start = ((), (), s32[]{:S(2)}) async-start(), calls=%async_computation.3 | async-start | bytes 8388608 | tf_op jit(solution)/shard_map/psum | solution.py:13
  531.2 2.6 copy-start.4
  531.2 2.6 copy-start.5
  531.2 2.7 copy-start.7
  533.8 253.3 %all-gather.7.cloned.1.call-start = ((), (), s32[]{:S(2)}) async-start(), calls=%async_computation.1 | async-start | bytes 2621440 | tf_op jit(solution)/shard_map/all_gather | solution.py:103
  534.0 4.5 copy-start.2
  765.4 196.2 %all-reduce.11.cloned.1.call-start = ((), (), s32[]{:S(2)}) async-start(), calls=%async_computation.2 | async-start | bytes 8388608 | tf_op jit(solution)/shard_map/psum | solution.py:13
  961.5 4.8 copy-start.1
Sparse Core Ops, SparseCore 0:
  14.1 401.0 all-reduce.14
  494.3 21.7 all-gather.4
  533.9 156.6 all-reduce.12
  765.5 21.5 all-gather.6
  804.9 156.6 all-reduce.10
where the time goes:
time: 1040 us; the launch traced here: 1030 us
  waiting for transfers between devices  691 us (66%)
  local copies, waits for them, and re-layouts  137 us (13%)
  matrix products  130 us (12%)
  other arithmetic  61.5 us (6%)
  between operations  13.9 us (1%)
    psum x3, waiting for transfers between devices, from_root(): return lax.psum(jnp.where(mine, array, jnp.zeros_like(array)), axis)  649 us
    dot_general x2, matrix products, local(): lax.dot_general(scaled, col_panel, (((1,), (1,)), ((), ())), preferred_el...  85.2 us
    unnamed x32, local copies, waits for them, and re-layouts  78.1 us
    all_gather x2, waiting for transfers between devices, local(): gathered = lax.all_gather(slab_cols, 'col', axis=2, tiled=True)  41.9 us
    dot_general x1, matrix products, local(): jnp.einsum('efij,efc->eicj', coupling, place_pair, precision=lax.Precisio...  24.8 us
  transfers between devices with their start and end apart: 5, of which 5 were waited for; matrix products, arithmetic and copies ran while one was open for 7% of the time, Pallas kernels for 0%

commit v1 on v0

v1 whole, which is shorter than its diff:
```python
import functools

import jax
import jax.numpy as jnp
from jax import lax
from jax.experimental import pallas as pl
from jax.experimental.pallas import tpu as pltpu
from jax.sharding import PartitionSpec as P

NB = 128
PW = 512
PANELS = 2
PB = PW // NB
MESH = pl.DeviceIdType.MESH
VMEM_LIMIT = 56 * 1024 * 1024
F32, BF16 = jnp.float32, jnp.bfloat16


def gather_kernel(rows, cols, split, keep_row, *refs):
    if keep_row:
        x_ref, g_ref, l_ref, swap_send, swap_recv, ring_send, ring_recv, row_send, row_recv = refs
    else:
        x_ref, g_ref, swap_send, swap_recv, ring_send, ring_recv = refs
    r, c = lax.axis_index("row"), lax.axis_index("col")
    s = lax.rem(r, cols)
    peer_row = r - s + c
    peer = (peer_row, s)
    stays = s == c

    def row_at(p):
        p = lax.rem(p + 2 * rows, rows)
        up = lax.div(p, rows // 2)
        return (1 - up) * (2 * p) + up * (2 * (rows - 1 - p) + 1)

    odd = lax.rem(r, 2)
    pos = (1 - odd) * lax.div(r, 2) + odd * (rows - 1 - lax.div(r, 2))
    beside = ((row_at(pos + 1), c), (row_at(pos - 1), c))

    barrier = pltpu.get_barrier_semaphore()
    for device in beside:
        pl.semaphore_signal(barrier, inc=1, device_id=device, device_id_type=MESH)
    greeted = 2
    if keep_row:
        for j in range(1, cols):
            pl.semaphore_signal(
                barrier, inc=1, device_id=(r, lax.rem(c + j, cols)), device_id_type=MESH
            )
        greeted += cols - 1

    @pl.when(jnp.logical_not(stays))
    def _():
        pl.semaphore_signal(barrier, inc=1, device_id=peer, device_id_type=MESH)
        pl.semaphore_wait(barrier, greeted + 1)

    @pl.when(stays)
    def _():
        pl.semaphore_wait(barrier, greeted)

    def source(half):
        return x_ref.at[c, half] if split else x_ref.at[half]

    def swap(half, slot):
        return pltpu.make_async_remote_copy(
            src_ref=source(half), dst_ref=g_ref.at[slot, half], send_sem=swap_send.at[half],
            recv_sem=swap_recv.at[half], device_id=peer, device_id_type=MESH,
        )

    def keep(half):
        return pltpu.make_async_copy(source(half), g_ref.at[r, half], swap_recv.at[half])

    @pl.when(stays)
    def _():
        for half in range(2):
            keep(half).start()

    @pl.when(jnp.logical_not(stays))
    def _():
        for half in range(2):
            swap(half, peer_row).start()

    def along_row(j, slot):
        return pltpu.make_async_remote_copy(
            src_ref=x_ref, dst_ref=l_ref.at[slot], send_sem=row_send.at[j], recv_sem=row_recv.at[j],
            device_id=(r, lax.rem(c + j, cols)), device_id_type=MESH,
        )

    if keep_row:
        own = pltpu.make_async_copy(x_ref, l_ref.at[c], row_recv.at[0])
        own.start()
        for j in range(1, cols):
            along_row(j, c).start()

    def ring(way, step):
        origin = row_at(pos - step) if way == 0 else row_at(pos + step)
        return pltpu.make_async_remote_copy(
            src_ref=g_ref.at[origin, way], dst_ref=g_ref.at[origin, way],
            send_sem=ring_send.at[way, step], recv_sem=ring_recv.at[way, step],
            device_id=beside[way], device_id_type=MESH,
        )

    def arrived(way, step):
        origin = row_at(pos - step - 1) if way == 0 else row_at(pos + step + 1)
        return pltpu.make_async_remote_copy(
            src_ref=g_ref.at[origin, way], dst_ref=g_ref.at[origin, way],
            send_sem=ring_send.at[way, step], recv_sem=ring_recv.at[way, step],
            device_id=beside[way], device_id_type=MESH,
        )

    for way in range(2):

        @pl.when(stays)
        def _():
            keep(way).wait()

        @pl.when(jnp.logical_not(stays))
        def _():
            swap(way, r).wait_recv()

        ring(way, 0).start()
    for step in range(1, rows - 1):
        for way in range(2):
            arrived(way, step - 1).wait_recv()
            ring(way, step).start()
    for way in range(2):
        arrived(way, rows - 2).wait_recv()
    for step in range(rows - 1):
        for way in range(2):
            ring(way, step).wait_send()

    @pl.when(jnp.logical_not(stays))
    def _():
        for half in range(2):
            swap(half, peer_row).wait_send()

    if keep_row:
        own.wait()
        for j in range(1, cols):
            along_row(j, lax.rem(c + cols - j, cols)).wait_recv()
            along_row(j, c).wait_send()


def gather(x, rows, cols, split, keep_row, identity):
    piece = x.shape[1:] if split else x.shape
    out_shape = [jax.ShapeDtypeStruct((rows,) + piece, x.dtype)]
    dma = pltpu.SemaphoreType.DMA
    scratch = [dma((2,)), dma((2,)), dma((2, rows - 1)), dma((2, rows - 1))]
    if keep_row:
        out_shape.append(jax.ShapeDtypeStruct((cols,) + piece, x.dtype))
        scratch += [dma((cols,)), dma((cols,))]
    moved = 2 * sum(o.size for o in out_shape)
    return pl.pallas_call(
        functools.partial(gather_kernel, rows, cols, split, keep_row),
        out_shape=out_shape,
        in_specs=[pl.BlockSpec(memory_space=pl.ANY)],
        out_specs=[pl.BlockSpec(memory_space=pl.ANY)] * len(out_shape),
        scratch_shapes=scratch,
        compiler_params=pltpu.CompilerParams(collective_id=identity, has_side_effects=True),
        cost_estimate=pl.CostEstimate(flops=0, bytes_accessed=20 * moved, transcendentals=0),
    )(x)


def face_kernel(slots, held, partner, self_info, own_ref, p0, p1, p2, p3, a_ref, c_ref, s_ref, v_ref, acc):
    e = pl.program_id(0)
    panel_slots = acc.shape[1] // NB
    acc[...] = a_ref[0]
    contract = (((0,), (0,)), ((), ()))

    def left(f):
        v, s, l = own_ref[0, f, 0], own_ref[0, f, 1], own_ref[0, f, 2]
        return jnp.concatenate([v, v, s, l], axis=0)

    def right(v, s, l):
        return jnp.concatenate([4.0 * v, -0.5 * s, -0.5 * v, 2.0 * l], axis=0)

    for f, p_ref in enumerate((p0, p1, p2, p3)):

        @pl.when(held[e * 4 + f] == 1)
        def _():
            z = right(p_ref[0, 0], p_ref[0, 1], p_ref[0, 2])
            c_ref[0, f] = lax.dot_general(left(f), z, contract, preferred_element_type=F32)
            for j in range(panel_slots):

                @pl.when(slots[e * 4 + f] == j)
                def _():
                    acc[:, j * NB : (j + 1) * NB] -= c_ref[0, f]

    @pl.when(self_info[0] == 1)
    def _():
        total = jnp.zeros((NB, NB), F32)
        for f in range(4):
            z = right(own_ref[0, f, 0], own_ref[0, f, 1], own_ref[0, f, 2])
            total += lax.dot_general(left(f), z, contract, preferred_element_type=F32)
        s_ref[0] = total
        for j in range(panel_slots):

            @pl.when(self_info[1 + e] == j)
            def _():
                acc[:, j * NB : (j + 1) * NB] += total

    v_ref[0] = acc[...].astype(BF16)


def faces(traces, partners, base, slots, held, partner, self_info):
    row_blocks, width = base.shape[0], base.shape[2]
    in_specs = [pl.BlockSpec((1, 4, 3, NB, NB), lambda e, *_: (e, 0, 0, 0, 0))]
    for f in range(4):
        in_specs.append(
            pl.BlockSpec((1, 3, NB, NB), lambda e, s, h, p, i, f=f: (p[e * 4 + f], 0, 0, 0))
        )
    in_specs.append(pl.BlockSpec((1, NB, width), lambda e, *_: (e, 0, 0)))
    return pl.pallas_call(
        face_kernel,
        grid_spec=pltpu.PrefetchScalarGridSpec(
            num_scalar_prefetch=4,
            grid=(row_blocks,),
            in_specs=in_specs,
            out_specs=[
                pl.BlockSpec((1, 4, NB, NB), lambda e, *_: (e, 0, 0, 0)),
                pl.BlockSpec((1, NB, NB), lambda e, *_: (e, 0, 0)),
                pl.BlockSpec((1, NB, width), lambda e, *_: (e, 0, 0)),
            ],
            scratch_shapes=[pltpu.VMEM((NB, width), F32)],
        ),
        out_shape=[
            jax.ShapeDtypeStruct((row_blocks, 4, NB, NB), F32),
            jax.ShapeDtypeStruct((row_blocks, NB, NB), F32),
            jax.ShapeDtypeStruct((row_blocks, NB, width), BF16),
        ],
        compiler_params=pltpu.CompilerParams(vmem_limit_bytes=VMEM_LIMIT),
    )(slots, held, partner, self_info, traces, partners, partners, partners, partners, base)


def panel_kernel(cols, transposed, kept, raw_ref, hi_ref, lo_ref, pivot_ref, out_ref):
    q, t = pl.program_id(0), pl.program_id(1)
    per = raw_ref.shape[2]
    blocks = pl.num_programs(1) * per
    first = q * blocks + t * per
    count = pl.num_programs(0) * blocks

    def masked(k, parts):
        return jnp.concatenate(
            [
                jnp.where(kept[k * count + first + i] == 1, parts[i], jnp.zeros_like(parts[i]))
                for i in range(per)
            ],
            axis=0,
        )

    def raw(k, i):
        pieces = []
        for b in range(k * PB, (k + 1) * PB):
            at = (b // cols) * NB
            pieces.append(raw_ref[0, b % cols, i, :, at : at + NB])
        return jnp.concatenate(pieces, axis=1)

    def scaled(k, v):
        w = jnp.dot(v, hi_ref[k], preferred_element_type=F32)
        return (w + jnp.dot(v, lo_ref[k], preferred_element_type=F32)).astype(BF16)

    v0 = masked(0, [raw(0, i) for i in range(per)])
    w0 = scaled(0, v0)
    taken = jnp.dot(w0, pivot_ref[...], preferred_element_type=F32)
    v1 = masked(
        1,
        [
            (raw(1, i).astype(F32) - taken[i * NB : (i + 1) * NB]).astype(BF16)
            for i in range(per)
        ],
    )
    if transposed:
        out_ref[:PW, :] = v0.T
        out_ref[PW:, :] = v1.T
    else:
        out_ref[:, :PW] = w0
        out_ref[:, PW:] = scaled(1, v1)


def panels(raw, kept, hi, lo, pivot_rows, transposed):
    groups, cols, row_blocks, _, width = raw.shape
    per = 4
    steps = row_blocks // per
    total = groups * row_blocks * NB
    whole = lambda shape: pl.BlockSpec(shape, lambda q, t, *_: (0,) * len(shape))
    if transposed:
        shape = (PANELS * PW, total)
        out_spec = pl.BlockSpec((PANELS * PW, per * NB), lambda q, t, *_: (0, q * steps + t))
    else:
        shape = (total, PANELS * PW)
        out_spec = pl.BlockSpec((per * NB, PANELS * PW), lambda q, t, *_: (q * steps + t, 0))
    return pl.pallas_call(
        functools.partial(panel_kernel, cols, transposed),
        grid_spec=pltpu.PrefetchScalarGridSpec(
            num_scalar_prefetch=1,
            grid=(groups, steps),
            in_specs=[
                pl.BlockSpec((1, cols, per, NB, width), lambda q, t, *_: (q, 0, t, 0, 0)),
                whole(hi.shape),
                whole(lo.shape),
                whole(pivot_rows.shape),
            ],
            out_specs=out_spec,
        ),
        out_shape=jax.ShapeDtypeStruct(shape, BF16),
        compiler_params=pltpu.CompilerParams(vmem_limit_bytes=VMEM_LIMIT),
    )(kept, raw, hi, lo, pivot_rows)


def update_kernel(groups, col_blocks, per, slots, held, self_info, a_ref, w_ref, v_ref, c_ref, s_ref, o_ref):
    t = pl.program_id(0)
    rows = per * NB
    per_group = col_blocks // groups
    w = w_ref[...]
    for h in range(groups):
        for a in range(0, per_group, 2):
            at = (h * per_group + a) * NB
            acc = jnp.dot(w, v_ref[:, at : at + 2 * NB], preferred_element_type=F32)
            for k in range(2):
                here = pl.ds((a + k) * groups + h, rows, stride=col_blocks)
                o_ref[here, :] = a_ref[here, :] - acc[:, k * NB : (k + 1) * NB]
    for i in range(per):
        e = t * per + i
        for f in range(4):

            @pl.when(held[e * 4 + f] == 1)
            def _():
                here = pl.ds(i * NB * col_blocks + slots[e * 4 + f], NB, stride=col_blocks)
                o_ref[here, :] = o_ref[here, :] - c_ref[i, f]

        @pl.when(self_info[0] == 1)
        def _():
            here = pl.ds(i * NB * col_blocks + self_info[1 + e], NB, stride=col_blocks)
            o_ref[here, :] = o_ref[here, :] + s_ref[i]


def update(front, w, v, coupling, self_terms, slots, held, self_info, groups, col_blocks):
    per = 2
    row_blocks = coupling.shape[0]
    wide = per * NB * col_blocks
    return pl.pallas_call(
        functools.partial(update_kernel, groups, col_blocks, per),
        grid_spec=pltpu.PrefetchScalarGridSpec(
            num_scalar_prefetch=3,
            grid=(row_blocks // per,),
            in_specs=[
                pl.BlockSpec((wide, NB), lambda t, *_: (t, 0)),
                pl.BlockSpec((per * NB, PANELS * PW), lambda t, *_: (t, 0)),
                pl.BlockSpec(v.shape, lambda t, *_: (0, 0)),
                pl.BlockSpec((per, 4, NB, NB), lambda t, *_: (t, 0, 0, 0)),
                pl.BlockSpec((per, NB, NB), lambda t, *_: (t, 0, 0)),
            ],
            out_specs=pl.BlockSpec((wide, NB), lambda t, *_: (t, 0)),
        ),
        out_shape=jax.ShapeDtypeStruct(front.shape, F32),
        compiler_params=pltpu.CompilerParams(vmem_limit_bytes=VMEM_LIMIT),
    )(slots, held, self_info, front, w, v, coupling, self_terms)


def inverse_matrix(order, kinds, diagonal, pair_terms):
    ids = jnp.arange(PW, dtype=jnp.int32)
    hot = order[:, :, None] == ids
    place = jnp.sum(jnp.where(hot, ids[None, :, None], 0), axis=1)
    diag = jnp.sum(jnp.where(hot, diagonal[:, :, None], 0.0), axis=1)
    starts = jnp.where(kinds == 1, pair_terms, 0.0)
    pair = jnp.sum(jnp.where(hot, starts[:, :, None], 0.0), axis=1)
    row, col = place[:, :, None], place[:, None, :]
    full = jnp.where(row == col, diag[:, :, None], 0.0)
    full = full + jnp.where(col == row + 1, pair[:, :, None], 0.0)
    full = full + jnp.where(row == col + 1, pair[:, None, :], 0.0)
    hi = full.astype(BF16)
    return hi, (full - hi.astype(F32)).astype(BF16)


def local(
    front_base,
    traces,
    adjacency,
    pivot_order,
    pivot_kind,
    inverse_diagonal,
    inverse_coupling,
    readers,
):
    rows, cols = lax.axis_size("row"), lax.axis_size("col")
    r, c = lax.axis_index("row"), lax.axis_index("col")
    row_blocks, col_blocks = front_base.shape[0], front_base.shape[3]
    groups = rows // cols
    panel_slots = -(-PANELS * PB // cols)
    width = panel_slots * NB

    own = traces.reshape(row_blocks, 4, 3, NB, NB)
    share = row_blocks * 4 // cols
    sent = traces.reshape(cols, 2, share // 2, 3 * NB, NB)
    (column_traces,) = gather(sent, rows, cols, True, False, 0)
    partners = column_traces.reshape(groups * row_blocks * 4, 3, NB, NB)

    elements = jnp.arange(row_blocks, dtype=jnp.int32) * rows + r
    neighbour = jnp.take(adjacency, elements, axis=0)
    opposite = jnp.array([1, 0, 3, 2], dtype=jnp.int32)
    here = neighbour % cols == c
    slots = (neighbour // cols).reshape(-1)
    partner = ((neighbour % rows // cols) * row_blocks + neighbour // rows) * 4 + opposite
    partner = jnp.where(here, partner, 0).reshape(-1)
    held = here.astype(jnp.int32).reshape(-1)
    self_here = (r % cols == c).astype(jnp.int32)
    self_info = jnp.concatenate([self_here[None], elements // cols])

    base = front_base[:, 0, :, :panel_slots, 0, :].reshape(row_blocks, NB, width)
    coupling, self_terms, raw = faces(own, partners, base, slots, held, partner, self_info)

    every = lax.all_gather(raw[0, :, :NB], ("row", "col"), axis=0, tiled=False)
    column_raw, row_raw = gather(
        raw.reshape(2, row_blocks * NB // 2, width), rows, cols, False, True, 1
    )
    ids = jnp.arange(rows * row_blocks, dtype=jnp.int32)
    kept = jnp.stack(
        [readers[k] * (ids >= (k + 1) * PB).astype(jnp.int32) for k in range(PANELS)]
    )
    by_row = kept.reshape(PANELS, row_blocks, rows)
    row_kept = lax.dynamic_index_in_dim(by_row, r, 2, keepdims=False)
    by_col = kept.reshape(PANELS, row_blocks, groups, cols)
    col_kept = lax.dynamic_index_in_dim(by_col, c, 3, keepdims=False).transpose(0, 2, 1)

    pivot = every.reshape(rows, cols, NB, NB)[PB : 2 * PB, :PB]
    pivot = pivot * kept[0, PB : 2 * PB].astype(BF16)[:, None, None, None]
    pivot_rows = pivot.transpose(1, 3, 0, 2).reshape(PW, PW)
    hi, lo = inverse_matrix(pivot_order, pivot_kind, inverse_diagonal, inverse_coupling)
    shape = (cols, row_blocks, NB, width)
    w = panels(row_raw.reshape((1,) + shape), row_kept.reshape(-1), hi, lo, pivot_rows, False)
    v = panels(column_raw.reshape((groups,) + shape), col_kept.reshape(-1), hi, lo, pivot_rows, True)

    front = front_base.reshape(row_blocks * NB * col_blocks, NB)
    out = update(front, w, v, coupling, self_terms, slots, held, self_info, groups, col_blocks)
    return out.reshape(front_base.shape)


def solution(mesh):
    in_specs = (
        P(None, "row", None, None, "col", None),
        P(None, "row", None, None, None, None),
        P(),
        P(),
        P(),
        P(),
        P(),
        P(),
    )
    out_specs = P(None, "row", None, None, "col", None)
    return jax.shard_map(local, mesh=mesh, in_specs=in_specs, out_specs=out_specs, check_vma=False)
```

time: 1040 us -> 434 us (0.42)
  waiting for transfers between devices: 691 us -> 0.02 us
  Pallas kernels: 0 us -> 394 us
  matrix products: 130 us -> 0 us
  local copies, waits for them, and re-layouts: 137 us -> 18.7 us
  other arithmetic: 61.5 us -> 5.1 us
    psum x3 -> x0, waiting for transfers between devices: 649 us -> none  [from_root(): return lax.psum(jnp.where(mine, array, jnp.zeros_like(array)), axis)]
    pallas_call x0 -> x6, Pallas kernels: none -> 394 us  [the longest x2 291 us: gather(): pl.pallas_call(functools.partial(gather_kernel, rows, cols, split, keep_r...]
    dot_general x5 -> x0, matrix products: 130 us -> none  [the longest x2 85.2 us: local(): lax.dot_general(scaled, col_panel, (((1,), (1,)), ((), ())), preferred_el...]
    unnamed x32 -> x12, local copies, waits for them, and re-layouts: 78.1 us -> 1.73 us
    all_gather x2 -> x1, waiting for transfers between devices: 41.9 us -> 0.01 us  [local(): every = lax.all_gather(raw[0, :, :NB], ('row', 'col'), axis=0, tiled=False)]
    another operation x6 -> x1, other arithmetic: 25.3 us -> 0.01 us  [local(): jnp.stack([readers[k] * (ids >= (k + 1) * PB).astype(jnp.int32) for k in...]
    gather x7 -> x1, local copies, waits for them, and re-layouts: 20.3 us -> 0.56 us  [local(): neighbour = jnp.take(adjacency, elements, axis=0)]
    unnamed x2 -> x0, other arithmetic: 12.1 us -> none
  transfers between devices with their start and end apart: 5 -> 1, of which waited for: 5 -> 0; matrix products, arithmetic and copies ran while one was open for 7% -> 1% of each run, Pallas kernels for 0% -> 29%
where the time goes in v1:
time: 434 us; the launch traced here: 431 us
  Pallas kernels  394 us (91%)
  local copies, waits for them, and re-layouts  18.7 us (4%)
  between operations  13.6 us (3%)
  other arithmetic  5.1 us (1%)
    pallas_call x2, Pallas kernels, gather(): pl.pallas_call(functools.partial(gather_kernel, rows, cols, split, keep_r...  291 us
    pallas_call x1, Pallas kernels, update(): pl.pallas_call(functools.partial(update_kernel, groups, col_blocks, per),...  62.5 us
    pallas_call x2, Pallas kernels, panels(): pl.pallas_call(functools.partial(panel_kernel, cols, transposed), grid_sp...  24.1 us
    pallas_call x1, Pallas kernels, faces(): pl.pallas_call(face_kernel, grid_spec=pltpu.PrefetchScalarGridSpec(num_sc...  16.4 us
  transfers between devices with their start and end apart: 1, of which 0 were waited for; matrix products, arithmetic and copies ran while one was open for 1% of the time, Pallas kernels for 29%

profile of v1, /device:TPU:0, one launch (start us, length us, event | category | flops | bytes accessed | tf_op | source)
XLA Modules:
  0.0 431.4 jit_solution(845586919996410280)
XLA Ops:
  6.6 0.7 add.116
  7.4 0.8 copy.18
  8.1 0.6 gather_fusion
  8.9 0.6 compare_convert_fusion.held
  9.4 0.6 compare_select_fusion.11
  10.0 8.3 %slice_reduce_fusion = f32[16,128,2,128]{3,2,1,0:T(2,128)S(1)} fusion(f32[16,1,128,32,1,128]{5,4,3,2,1,0:T(1,128)} %param.9), kind=kLoop, calls=%fused_computation.7 | loop fusion | bytes 4194304 | tf_op jit(solution)/shard_map/slice | solution.py:407
  18.3 2.7 reshape_squeeze.3.a_ref
  21.0 167.7 %shard_map.91 = bf16[8,2,8,384,128]{4,3,2,1,0:T(8,128)(2,1)} custom-call(bf16[4,2,8,384,128]{4,3,2,1,0:T(8,128)(2,1)} %bitcast.34), custom_call_target="tpu_custom_call" | custom-call | bytes 251658240 | tf_op jit(solution)/shard_map/pallas_call | solution.py:151
  188.7 0.6 pad_add_fusion.self_info
  189.4 16.4 %shard_map.92 = (f32[16,4,128,128]{3,2,1,0:T(8,128)}, f32[16,128,128]{2,1,0:T(8,128)}, bf16[16,128,256]{2,1,0:T(8,128)(2,1)}) custom-call(s32[64]{0:T(128)} %get-tuple-element.25.slots, s32[64]{0:T(128)} %compare_convert_fusion.held, s32[64]{0:T(128)} %get-tuple-element.24.partner, s32[17]{0:T(128)} %pad_add_fusion.self_info, ...), custom_call_target="tpu_custom_call" | custom-call | tf_op jit(solution)/shard_map/pallas_call | solution.py:211
  205.8 1.4 slice.25
  207.5 0.6 reshape.116.kept
  208.6 0.7 reshape.123.kept
  209.3 123.4 %shard_map.93 = (bf16[8,2,1024,256]{3,2,1,0:T(8,128)(2,1)}, bf16[4,2,1024,256]{3,2,1,0:T(8,128)(2,1)}) custom-call(bf16[2,1024,256]{2,1,0:T(8,128)(2,1)} %bitcast.42), custom_call_target="tpu_custom_call" | custom-call | bytes 251658240 | tf_op jit(solution)/shard_map/pallas_call | solution.py:151
  332.6 0.3 select_reduce_fusion.2
  333.0 0.6 select_reduce_fusion.1
  333.7 1.8 subtract_convert_fusion
  335.5 1.1 slice.31
  336.5 0.3 copy.19
  336.9 0.3 broadcast_multiply_fusion
  337.2 0.9 copy.25
  338.1 9.9 %shard_map.94.w_ref = bf16[2048,1024]{1,0:T(8,128)(2,1)} custom-call(s32[32]{0:T(128)} %reshape.116.kept, bf16[1,4,16,128,256]{4,3,2,1,0:T(8,128)(2,1)} %bitcast.39, bf16[2,512,512]{2,1,0:T(8,128)(2,1)} %get-tuple-element.20.hi_ref, bf16[2,512,512]{2,1,0:T(8,128)(2,1)} %get-tuple-element.19.lo_ref, bf16[512,512]{1,0:T(8,128)(2,1)} %bitcast.37), custom_call_target="tpu_custom_call" | custom-call | tf_op jit(solution)/shard_map/pallas_call | solution.py:290
  348.0 14.1 %shard_map.95.v_ref = bf16[1024,4096]{1,0:T(8,128)(2,1)} custom-call(s32[64]{0:T(128)} %reshape.123.kept, bf16[2,4,16,128,256]{4,3,2,1,0:T(8,128)(2,1)} %bitcast.36, bf16[2,512,512]{2,1,0:T(8,128)(2,1)} %get-tuple-element.20.hi_ref, bf16[2,512,512]{2,1,0:T(8,128)(2,1)} %get-tuple-element.19.lo_ref, bf16[512,512]{1,0:T(8,128)(2,1)} %bitcast.38), custom_call_target="tpu_custom_call" | custom-call | tf_op jit(solution)/shard_map/pallas_call | solution.py:290
  362.1 62.5 %shard_map.96 = f32[65536,128]{1,0:T(8,128)} custom-call(s32[64]{0:T(128)} %get-tuple-element.25.slots, s32[64]{0:T(128)} %compare_convert_fusion.held, s32[17]{0:T(128)} %pad_add_fusion.self_info, f32[65536,128]{1,0:T(8,128)} %bitcast.33, bf16[2048,1024]{1,0:T(8,128)(2,1)} %shard_map.94.w_ref, bf16[1024,4096]{1,0:T(8,128)(2,1)} %shard_map.95.v_ref, ...), custom_call_target="tpu_custom_call" | custom-call | tf_op jit(solution)/shard_map/pallas_call | solution.py:339
  (32 shorter events, 1.2 us)
Async XLA Ops:
  6.5 328.9 %all-gather.2.cloned.1.call-start = ((), (), s32[]{:S(2)}) async-start(), calls=%async_computation | async-start | bytes 1081344 | tf_op jit(solution)/shard_map/all_gather | solution.py:410
  189.4 17.8 %copy-start.4 = (s32[2,128]{1,0:T(2,128)S(1)}, s32[2,128]{1,0:T(2,128)}, u32[]{:S(2)}) copy-start(s32[2,128]{1,0:T(2,128)} %param.16) | copy-start | bytes 3076
  189.4 143.3 %copy-start = (s32[2,512]{1,0:T(2,128)S(1)}, s32[2,512]{1,0:T(2,128)}, u32[]{:S(2)}) copy-start(s32[2,512]{1,0:T(2,128)} %param.12) | copy-start | bytes 12292
  189.4 143.6 %copy-start.1 = (f32[2,512]{1,0:T(2,128)S(1)}, f32[2,512]{1,0:T(2,128)}, u32[]{:S(2)}) copy-start(f32[2,512]{1,0:T(2,128)} %param.15) | copy-start | bytes 12292
  189.4 143.6 %copy-start.2 = (s32[2,512]{1,0:T(2,128)S(1)}, s32[2,512]{1,0:T(2,128)}, u32[]{:S(2)}) copy-start(s32[2,512]{1,0:T(2,128)} %param.13) | copy-start | bytes 12292
  189.4 143.6 %copy-start.3 = (f32[2,512]{1,0:T(2,128)S(1)}, f32[2,512]{1,0:T(2,128)}, u32[]{:S(2)}) copy-start(f32[2,512]{1,0:T(2,128)} %param.14) | copy-start | bytes 12292
Sparse Core Ops, SparseCore 0:
  207.3 75.8 all-gather.1

commit v2 on v1

v2 whole, which is shorter than its diff:
```python
import functools

import jax
import jax.numpy as jnp
from jax import lax
from jax.experimental import pallas as pl
from jax.experimental.pallas import tpu as pltpu
from jax.sharding import PartitionSpec as P

NB = 128
PW = 512
PANELS = 2
PB = PW // NB
MESH = pl.DeviceIdType.MESH
VMEM_LIMIT = 56 * 1024 * 1024
F32, BF16 = jnp.float32, jnp.bfloat16


def gather_kernel(rows, cols, parts, split, keep_row, *refs):
    if keep_row:
        (x_ref, y_ref, g_ref, l_ref, t_ref, swap_send, swap_recv, ring_send, ring_recv,
         row_send, row_recv, turn_send, turn_recv) = refs
    else:
        x_ref, g_ref, swap_send, swap_recv, ring_send, ring_recv = refs
    groups = rows // cols
    r, c = lax.axis_index("row"), lax.axis_index("col")
    s = lax.rem(r, cols)
    h = lax.div(r, cols)
    peer_row = r - s + c
    peer = (peer_row, s)
    stays = s == c

    def row_at(p):
        p = lax.rem(p + 2 * rows, rows)
        up = lax.div(p, rows // 2)
        return (1 - up) * (2 * p) + up * (2 * (rows - 1 - p) + 1)

    odd = lax.rem(r, 2)
    pos = (1 - odd) * lax.div(r, 2) + odd * (rows - 1 - lax.div(r, 2))
    beside = ((row_at(pos + 1), c), (row_at(pos - 1), c))
    pieces = [(way, part) for part in range(parts) for way in range(2)]

    barrier = pltpu.get_barrier_semaphore()
    for device in beside:
        pl.semaphore_signal(barrier, inc=1, device_id=device, device_id_type=MESH)
    greeted = 2
    if keep_row:
        for j in range(1, cols):
            pl.semaphore_signal(
                barrier, inc=1, device_id=(r, lax.rem(c + j, cols)), device_id_type=MESH
            )
        for j in range(1, groups):
            turned = lax.rem(h + j, groups) * cols + c
            pl.semaphore_signal(barrier, inc=1, device_id=(turned, s), device_id_type=MESH)
        greeted += cols - 1 + groups - 1

    @pl.when(jnp.logical_not(stays))
    def _():
        pl.semaphore_signal(barrier, inc=1, device_id=peer, device_id_type=MESH)
        pl.semaphore_wait(barrier, greeted + 1)

    @pl.when(stays)
    def _():
        pl.semaphore_wait(barrier, greeted)

    def source(way, part):
        return x_ref.at[c, way, part] if split else x_ref.at[way, part]

    def swap(way, part, slot):
        return pltpu.make_async_remote_copy(
            src_ref=source(way, part), dst_ref=g_ref.at[slot, way, part],
            send_sem=swap_send.at[way, part], recv_sem=swap_recv.at[way, part],
            device_id=peer, device_id_type=MESH,
        )

    def keep(way, part):
        return pltpu.make_async_copy(
            source(way, part), g_ref.at[r, way, part], swap_recv.at[way, part]
        )

    @pl.when(stays)
    def _():
        for piece in pieces:
            keep(*piece).start()

    @pl.when(jnp.logical_not(stays))
    def _():
        for piece in pieces:
            swap(*piece, peer_row).start()

    def along_row(j, slot):
        return pltpu.make_async_remote_copy(
            src_ref=x_ref, dst_ref=l_ref.at[slot], send_sem=row_send.at[j], recv_sem=row_recv.at[j],
            device_id=(r, lax.rem(c + j, cols)), device_id_type=MESH,
        )

    def turn(j, slot):
        k = lax.rem(h + j, groups)
        return pltpu.make_async_remote_copy(
            src_ref=y_ref.at[k], dst_ref=t_ref.at[slot], send_sem=turn_send.at[j],
            recv_sem=turn_recv.at[j], device_id=(k * cols + c, s), device_id_type=MESH,
        )

    def turn_kept():
        return pltpu.make_async_copy(y_ref.at[h], t_ref.at[h], turn_recv.at[0])

    if keep_row:
        own = pltpu.make_async_copy(x_ref, l_ref.at[c], row_recv.at[0])
        own.start()
        for j in range(1, cols):
            along_row(j, c).start()
        for j in range(1, groups):
            turn(j, h).start()

        @pl.when(stays)
        def _():
            turn_kept().start()

        @pl.when(jnp.logical_not(stays))
        def _():
            turn(0, h).start()

    def ring(way, part, step, behind):
        origin = row_at(pos - step - behind) if way == 0 else row_at(pos + step + behind)
        return pltpu.make_async_remote_copy(
            src_ref=g_ref.at[origin, way, part], dst_ref=g_ref.at[origin, way, part],
            send_sem=ring_send.at[way, part, step], recv_sem=ring_recv.at[way, part, step],
            device_id=beside[way], device_id_type=MESH,
        )

    for way, part in pieces:

        @pl.when(stays)
        def _():
            keep(way, part).wait()

        @pl.when(jnp.logical_not(stays))
        def _():
            swap(way, part, r).wait_recv()

        ring(way, part, 0, 0).start()
    for step in range(1, rows - 1):
        for way, part in pieces:
            ring(way, part, step - 1, 1).wait_recv()
            ring(way, part, step, 0).start()
    for way, part in pieces:
        ring(way, part, rows - 2, 1).wait_recv()
    for step in range(rows - 1):
        for way, part in pieces:
            ring(way, part, step, 0).wait_send()

    @pl.when(jnp.logical_not(stays))
    def _():
        for piece in pieces:
            swap(*piece, peer_row).wait_send()

    if keep_row:
        own.wait()
        for j in range(1, cols):
            along_row(j, lax.rem(c + cols - j, cols)).wait_recv()
            along_row(j, c).wait_send()
        for j in range(1, groups):
            turn(j, lax.rem(h + groups - j, groups)).wait_recv()
            turn(j, h).wait_send()

        @pl.when(stays)
        def _():
            turn_kept().wait()

        @pl.when(jnp.logical_not(stays))
        def _():
            turn(0, h).wait_recv()
            turn(0, h).wait_send()


def gather(x, rows, cols, split, identity, turned=None):
    piece = x.shape[1:] if split else x.shape
    parts = piece[1]
    out_shape = [jax.ShapeDtypeStruct((rows,) + piece, x.dtype)]
    dma = pltpu.SemaphoreType.DMA
    scratch = [dma((2, parts)), dma((2, parts)), dma((2, parts, rows - 1)), dma((2, parts, rows - 1))]
    operands = [x]
    keep_row = turned is not None
    if keep_row:
        out_shape.append(jax.ShapeDtypeStruct((cols,) + piece, x.dtype))
        out_shape.append(jax.ShapeDtypeStruct(turned.shape, turned.dtype))
        scratch += [dma((cols,)), dma((cols,)), dma((rows // cols,)), dma((rows // cols,))]
        operands.append(turned)
    moved = 2 * sum(o.size for o in out_shape)
    return pl.pallas_call(
        functools.partial(gather_kernel, rows, cols, parts, split, keep_row),
        out_shape=out_shape,
        in_specs=[pl.BlockSpec(memory_space=pl.ANY)] * len(operands),
        out_specs=[pl.BlockSpec(memory_space=pl.ANY)] * len(out_shape),
        scratch_shapes=scratch,
        compiler_params=pltpu.CompilerParams(collective_id=identity, has_side_effects=True),
        cost_estimate=pl.CostEstimate(flops=0, bytes_accessed=20 * moved, transcendentals=0),
    )(*operands)


def face_kernel(slots, held, partner, self_info, place, own_ref, p0, p1, p2, p3, a_ref, c_ref, s_ref, v_ref, t_ref, acc):
    e = pl.program_id(0)
    panel_slots = acc.shape[1] // NB
    acc[...] = a_ref[0]
    contract = (((0,), (0,)), ((), ()))

    def left(f):
        v, s, l = own_ref[0, f, 0], own_ref[0, f, 1], own_ref[0, f, 2]
        return jnp.concatenate([v, v, s, l], axis=0)

    def right(v, s, l):
        return jnp.concatenate([4.0 * v, -0.5 * s, -0.5 * v, 2.0 * l], axis=0)

    @pl.when(e == 0)
    def _():
        t_ref[...] = jnp.zeros_like(t_ref)

    for f, p_ref in enumerate((p0, p1, p2, p3)):
        wanted = held[e * 4 + f] == 1
        if f % 2:
            wanted = jnp.logical_and(wanted, slots[e * 4 + f] < panel_slots)

        @pl.when(wanted)
        def _():
            z = right(p_ref[0, 0], p_ref[0, 1], p_ref[0, 2])
            block = lax.dot_general(left(f), z, contract, preferred_element_type=F32)
            if f % 2 == 0:
                c_ref[0, f // 2] = block

                @pl.when(place[e * 2 + f // 2] >= 0)
                def _():
                    t_ref[place[e * 2 + f // 2]] = block.T.astype(BF16)

            for j in range(panel_slots):

                @pl.when(slots[e * 4 + f] == j)
                def _():
                    acc[:, j * NB : (j + 1) * NB] -= block

    @pl.when(self_info[0] == 1)
    def _():
        total = jnp.zeros((NB, NB), F32)
        for f in range(4):
            z = right(own_ref[0, f, 0], own_ref[0, f, 1], own_ref[0, f, 2])
            total += lax.dot_general(left(f), z, contract, preferred_element_type=F32)
        s_ref[0] = total
        for j in range(panel_slots):

            @pl.when(self_info[1 + e] == j)
            def _():
                acc[:, j * NB : (j + 1) * NB] += total

    v_ref[0] = acc[...].astype(BF16)


def faces(traces, partners, base, slots, held, partner, self_info, place, room):
    row_blocks, width = base.shape[0], base.shape[2]
    in_specs = [pl.BlockSpec((1, 4, 3, NB, NB), lambda e, *_: (e, 0, 0, 0, 0))]
    for f in range(4):
        in_specs.append(
            pl.BlockSpec((1, 3, NB, NB), lambda e, s, h, p, i, t, f=f: (p[e * 4 + f], 0, 0, 0))
        )
    in_specs.append(pl.BlockSpec((1, NB, width), lambda e, *_: (e, 0, 0)))
    return pl.pallas_call(
        face_kernel,
        grid_spec=pltpu.PrefetchScalarGridSpec(
            num_scalar_prefetch=5,
            grid=(row_blocks,),
            in_specs=in_specs,
            out_specs=[
                pl.BlockSpec((1, 2, NB, NB), lambda e, *_: (e, 0, 0, 0)),
                pl.BlockSpec((1, NB, NB), lambda e, *_: (e, 0, 0)),
                pl.BlockSpec((1, NB, width), lambda e, *_: (e, 0, 0)),
                pl.BlockSpec((room, NB, NB), lambda e, *_: (0, 0, 0)),
            ],
            scratch_shapes=[pltpu.VMEM((NB, width), F32)],
        ),
        out_shape=[
            jax.ShapeDtypeStruct((row_blocks, 2, NB, NB), F32),
            jax.ShapeDtypeStruct((row_blocks, NB, NB), F32),
            jax.ShapeDtypeStruct((row_blocks, NB, width), BF16),
            jax.ShapeDtypeStruct((room, NB, NB), BF16),
        ],
        compiler_params=pltpu.CompilerParams(vmem_limit_bytes=VMEM_LIMIT),
    )(slots, held, partner, self_info, place, traces, partners, partners, partners, partners, base)


def panel_kernel(cols, transposed, kept, raw_ref, hi_ref, lo_ref, pivot_ref, out_ref):
    q, t = pl.program_id(0), pl.program_id(1)
    per = raw_ref.shape[2]
    blocks = pl.num_programs(1) * per
    first = q * blocks + t * per
    count = pl.num_programs(0) * blocks

    def masked(k, parts):
        return jnp.concatenate(
            [
                jnp.where(kept[k * count + first + i] == 1, parts[i], jnp.zeros_like(parts[i]))
                for i in range(per)
            ],
            axis=0,
        )

    def raw(k, i):
        pieces = []
        for b in range(k * PB, (k + 1) * PB):
            at = (b // cols) * NB
            pieces.append(raw_ref[0, b % cols, i, :, at : at + NB])
        return jnp.concatenate(pieces, axis=1)

    def scaled(k, v):
        w = jnp.dot(v, hi_ref[k], preferred_element_type=F32)
        return (w + jnp.dot(v, lo_ref[k], preferred_element_type=F32)).astype(BF16)

    v0 = masked(0, [raw(0, i) for i in range(per)])
    w0 = scaled(0, v0)
    taken = jnp.dot(w0, pivot_ref[...], preferred_element_type=F32)
    v1 = masked(
        1,
        [
            (raw(1, i).astype(F32) - taken[i * NB : (i + 1) * NB]).astype(BF16)
            for i in range(per)
        ],
    )
    if transposed:
        out_ref[:PW, :] = v0.T
        out_ref[PW:, :] = v1.T
    else:
        out_ref[:, :PW] = w0
        out_ref[:, PW:] = scaled(1, v1)


def panels(raw, kept, hi, lo, pivot_rows, transposed):
    groups, cols, row_blocks, _, width = raw.shape
    per = 4
    steps = row_blocks // per
    total = groups * row_blocks * NB
    whole = lambda shape: pl.BlockSpec(shape, lambda q, t, *_: (0,) * len(shape))
    if transposed:
        shape = (PANELS * PW, total)
        out_spec = pl.BlockSpec((PANELS * PW, per * NB), lambda q, t, *_: (0, q * steps + t))
    else:
        shape = (total, PANELS * PW)
        out_spec = pl.BlockSpec((per * NB, PANELS * PW), lambda q, t, *_: (q * steps + t, 0))
    return pl.pallas_call(
        functools.partial(panel_kernel, cols, transposed),
        grid_spec=pltpu.PrefetchScalarGridSpec(
            num_scalar_prefetch=1,
            grid=(groups, steps),
            in_specs=[
                pl.BlockSpec((1, cols, per, NB, width), lambda q, t, *_: (q, 0, t, 0, 0)),
                whole(hi.shape),
                whole(lo.shape),
                whole(pivot_rows.shape),
            ],
            out_specs=out_spec,
        ),
        out_shape=jax.ShapeDtypeStruct(shape, BF16),
        compiler_params=pltpu.CompilerParams(vmem_limit_bytes=VMEM_LIMIT),
    )(kept, raw, hi, lo, pivot_rows)


def update_kernel(groups, per, slots, held, self_info, a_ref, w_ref, v_ref, c_ref, d_ref, s_ref, o_ref):
    t = pl.program_id(0)
    rows, col_blocks = a_ref.shape[:2]
    per_group = col_blocks // groups
    some = 8 // groups
    w = w_ref[...]
    for first in range(0, col_blocks, 8):
        parts = []
        for h in range(groups):
            at = (h * per_group + first // groups) * NB
            parts.append(
                jnp.dot(w, v_ref[:, at : at + some * NB], preferred_element_type=F32)
            )
        slabs = [
            parts[j % groups][:, (j // groups) * NB : (j // groups + 1) * NB] for j in range(8)
        ]
        turned = jnp.transpose(jnp.stack(slabs, axis=0), (1, 0, 2))
        o_ref[:, first : first + 8, :] = a_ref[:, first : first + 8, :] - turned
    flat = o_ref.reshape(rows * col_blocks, NB)
    for i in range(per):
        e = t * per + i
        for f in range(4):

            @pl.when(held[e * 4 + f] == 1)
            def _():
                here = pl.ds(i * NB * col_blocks + slots[e * 4 + f], NB, stride=col_blocks)
                block = d_ref[i, f // 2].astype(F32) if f % 2 else c_ref[i, f // 2]
                flat[here, :] = flat[here, :] - block

        @pl.when(self_info[0] == 1)
        def _():
            here = pl.ds(i * NB * col_blocks + self_info[1 + e], NB, stride=col_blocks)
            flat[here, :] = flat[here, :] + s_ref[i]


def update(front, w, v, even, odd, self_terms, slots, held, self_info, groups):
    per = 2
    row_blocks, col_blocks = even.shape[0], front.shape[1]
    return pl.pallas_call(
        functools.partial(update_kernel, groups, per),
        grid_spec=pltpu.PrefetchScalarGridSpec(
            num_scalar_prefetch=3,
            grid=(row_blocks // per,),
            in_specs=[
                pl.BlockSpec((per * NB, col_blocks, NB), lambda t, *_: (t, 0, 0)),
                pl.BlockSpec((per * NB, PANELS * PW), lambda t, *_: (t, 0)),
                pl.BlockSpec(v.shape, lambda t, *_: (0, 0)),
                pl.BlockSpec((per, 2, NB, NB), lambda t, *_: (t, 0, 0, 0)),
                pl.BlockSpec((per, 2, NB, NB), lambda t, *_: (t, 0, 0, 0)),
                pl.BlockSpec((per, NB, NB), lambda t, *_: (t, 0, 0)),
            ],
            out_specs=pl.BlockSpec((per * NB, col_blocks, NB), lambda t, *_: (t, 0, 0)),
        ),
        out_shape=jax.ShapeDtypeStruct(front.shape, F32),
        compiler_params=pltpu.CompilerParams(vmem_limit_bytes=VMEM_LIMIT),
    )(slots, held, self_info, front, w, v, even, odd, self_terms)


def inverse_matrix(order, kinds, diagonal, pair_terms):
    ids = jnp.arange(PW, dtype=jnp.int32)
    hot = (order[:, :, None] == ids).astype(F32)
    starts = jnp.where(kinds == 1, pair_terms, 0.0)
    places = jnp.broadcast_to(ids.astype(F32), order.shape)
    wanted = jnp.stack([places, diagonal, starts], axis=1)
    found = jnp.einsum("kdi,kij->kdj", wanted, hot, precision=lax.Precision.HIGHEST)
    place, diag, pair = jnp.round(found[:, 0]).astype(jnp.int32), found[:, 1], found[:, 2]
    row, col = place[:, :, None], place[:, None, :]
    full = jnp.where(row == col, diag[:, :, None], 0.0)
    full = full + jnp.where(col == row + 1, pair[:, :, None], 0.0)
    full = full + jnp.where(row == col + 1, pair[:, None, :], 0.0)
    hi = full.astype(BF16)
    return hi, (full - hi.astype(F32)).astype(BF16)


def local(
    front_base,
    traces,
    adjacency,
    pivot_order,
    pivot_kind,
    inverse_diagonal,
    inverse_coupling,
    readers,
):
    rows, cols = lax.axis_size("row"), lax.axis_size("col")
    r, c = lax.axis_index("row"), lax.axis_index("col")
    row_blocks, col_blocks = front_base.shape[0], front_base.shape[3]
    groups = rows // cols
    panel_slots = -(-PANELS * PB // cols)
    width = panel_slots * NB

    own = traces.reshape(row_blocks, 4, 3, NB, NB)
    parts = 2
    first_even = own[0, 0::2]
    chosen = jnp.concatenate([own[:, 1::2].reshape(-1, 3, NB, NB), first_even])
    count = chosen.shape[0]
    while count * 3 * NB % (cols * 2 * parts * 16):
        count += 1
    chosen = jnp.pad(chosen, ((0, count - chosen.shape[0]), (0, 0), (0, 0), (0, 0)))
    sent = chosen.reshape(cols, 2, parts, -1, NB)
    (column_traces,) = gather(sent, rows, cols, True, 0)
    partners = column_traces.reshape(groups * count, 3, NB, NB)

    elements = jnp.arange(row_blocks, dtype=jnp.int32) * rows + r
    neighbour = jnp.take(adjacency, elements, axis=0)
    here = neighbour % cols == c
    slots = (neighbour // cols).reshape(-1)
    faces_at = jnp.arange(4, dtype=jnp.int32)
    meets = jnp.where(
        faces_at % 2 == 0,
        (neighbour // rows) * 2 + faces_at // 2,
        row_blocks * 2 + faces_at // 2,
    )
    partner = (neighbour % rows // cols) * count + meets
    needed = here & ((faces_at % 2 == 0) | (neighbour < panel_slots * cols))
    partner = jnp.where(needed, partner, 0).reshape(-1)
    held = here.astype(jnp.int32).reshape(-1)
    self_here = (r % cols == c).astype(jnp.int32)
    self_info = jnp.concatenate([self_here[None], elements // cols])

    cap = 3 * row_blocks // 4
    toward = adjacency.reshape(row_blocks, rows, 4)[:, :, 0::2] % rows
    toward = toward.transpose(0, 2, 1).reshape(row_blocks * 2, rows)
    goes = (toward[:, :, None] == jnp.arange(rows, dtype=jnp.int32)).astype(jnp.int32)
    earlier = jnp.cumsum(goes, axis=0) - goes
    rank = jnp.sum(earlier * goes, axis=2)
    crowded = jnp.any(rank >= cap)
    my_rank = lax.dynamic_index_in_dim(rank, r, 1, keepdims=False)
    my_even = neighbour[:, 0::2].reshape(-1)
    here_even = here[:, 0::2].reshape(-1)
    place = jnp.where(here_even & (my_rank < cap), my_even % rows // cols * cap + my_rank, -1)

    base = front_base[:, 0, :, :panel_slots, 0, :].reshape(row_blocks, NB, width)
    even, self_terms, raw, outgoing = faces(
        own, partners, base, slots, held, partner, self_info, place, groups * cap
    )

    every = lax.all_gather(raw[0, :, :NB], ("row", "col"), axis=0, tiled=False)
    column_raw, row_raw, incoming = gather(
        raw.reshape(2, 4, row_blocks * NB // 8, width), rows, cols, False, 1,
        outgoing.reshape(groups, cap, NB, NB),
    )

    my_odd = neighbour[:, 1::2]
    source_face = my_odd // rows * 2 + jnp.arange(2, dtype=jnp.int32)

    def from_places():
        at = (my_odd % rows // cols) * cap + rank[source_face, my_odd % rows]
        return jnp.take(incoming.reshape(groups * cap, NB, NB), at, axis=0, mode="clip")

    def from_all():
        dense = even.reshape(row_blocks * 2, NB, NB).transpose(0, 2, 1).astype(BF16)
        got = []
        for shift in range(groups):
            moves = [
                ((h * cols + a) * cols + b, ((h + shift) % groups * cols + b) * cols + a)
                for h in range(groups)
                for a in range(cols)
                for b in range(cols)
            ]
            got.append(lax.ppermute(dense, ("row", "col"), moves))
        shift = (r // cols - my_odd % rows // cols) % groups
        return jnp.stack(got)[shift, source_face]

    odd = lax.cond(crowded, from_all, from_places)

    ids = jnp.arange(rows * row_blocks, dtype=jnp.int32)
    kept = jnp.stack(
        [readers[k] * (ids >= (k + 1) * PB).astype(jnp.int32) for k in range(PANELS)]
    )
    by_row = kept.reshape(PANELS, row_blocks, rows)
    row_kept = lax.dynamic_index_in_dim(by_row, r, 2, keepdims=False)
    by_col = kept.reshape(PANELS, row_blocks, groups, cols)
    col_kept = lax.dynamic_index_in_dim(by_col, c, 3, keepdims=False).transpose(0, 2, 1)

    pivot = every.reshape(rows, cols, NB, NB)[PB : 2 * PB, :PB]
    pivot = pivot * kept[0, PB : 2 * PB].astype(BF16)[:, None, None, None]
    pivot_rows = pivot.transpose(1, 3, 0, 2).reshape(PW, PW)
    hi, lo = inverse_matrix(pivot_order, pivot_kind, inverse_diagonal, inverse_coupling)
    shape = (cols, row_blocks, NB, width)
    w = panels(row_raw.reshape((1,) + shape), row_kept.reshape(-1), hi, lo, pivot_rows, False)
    v = panels(column_raw.reshape((groups,) + shape), col_kept.reshape(-1), hi, lo, pivot_rows, True)

    front = front_base.reshape(row_blocks * NB, col_blocks, NB)
    out = update(front, w, v, even, odd, self_terms, slots, held, self_info, groups)
    return out.reshape(front_base.shape)


def solution(mesh):
    in_specs = (
        P(None, "row", None, None, "col", None),
        P(None, "row", None, None, None, None),
        P(),
        P(),
        P(),
        P(),
        P(),
        P(),
    )
    out_specs = P(None, "row", None, None, "col", None)
    return jax.shard_map(local, mesh=mesh, in_specs=in_specs, out_specs=out_specs, check_vma=False)
```

time: 434 us -> 358 us (0.82)
  Pallas kernels: 394 us -> 301 us
  local copies, waits for them, and re-layouts: 18.7 us -> 30.9 us
    pallas_call x3, Pallas kernels: 354 us -> 261 us  [the longest x2 223 us: gather(): pl.pallas_call(functools.partial(gather_kernel, rows, cols, parts, split,...]
  transfers between devices with their start and end apart: 1 -> 1, of which waited for: 0 -> 0; matrix products, arithmetic and copies ran while one was open for 1% -> 2% of each run, Pallas kernels for 29% -> 38%
where the time goes in v2:
time: 358 us; the launch traced here: 357 us
  Pallas kernels  301 us (84%)
  local copies, waits for them, and re-layouts  30.9 us (9%)
  between operations  14.3 us (4%)
  other arithmetic  9.27 us (3%)
    pallas_call x2, Pallas kernels, gather(): pl.pallas_call(functools.partial(gather_kernel, rows, cols, parts, split,...  223 us
    pallas_call x1, Pallas kernels, update(): pl.pallas_call(functools.partial(update_kernel, groups, per), grid_spec=p...  37.2 us
    pallas_call x2, Pallas kernels, panels(): pl.pallas_call(functools.partial(panel_kernel, cols, transposed), grid_sp...  24.1 us
    pallas_call x1, Pallas kernels, faces(): pl.pallas_call(face_kernel, grid_spec=pltpu.PrefetchScalarGridSpec(num_sc...  16.6 us
    slice x1, local copies, waits for them, and re-layouts, local(): front_base[:, 0, :, :panel_slots, 0, :].reshape(row_blocks, NB, width)  9.58 us
  transfers between devices with their start and end apart: 1, of which 0 were waited for; matrix products, arithmetic and copies ran while one was open for 2% of the time, Pallas kernels for 38%

profile of v2, /device:TPU:0, one launch (start us, length us, event | category | flops | bytes accessed | tf_op | source)
XLA Modules:
  0.0 356.6 jit_solution(11233959200619206970)
XLA Ops:
  6.6 0.8 reshape.165
  7.4 0.8 copy.42
  9.0 0.9 slice_bitcast_fusion
  9.9 2.1 slice.54
  12.4 0.7 fusion.53
  14.0 9.6 %slice_reduce_fusion = f32[16,128,2,128]{3,2,1,0:T(2,128)} fusion(f32[16,1,128,32,1,128]{5,4,3,2,1,0:T(1,128)} %param.10), kind=kLoop, calls=%fused_computation.53 | loop fusion | bytes 4194304 | tf_op jit(solution)/shard_map/slice | solution.py:495
  23.5 4.0 %reshape_squeeze.3.a_ref = f32[16,128,256]{2,1,0:T(8,128)} reshape(f32[16,128,2,128]{3,2,1,0:T(2,128)} %slice_reduce_fusion) | data formatting | bytes 4194304 | tf_op jit(solution)/shard_map/reshape;squeeze | solution.py:495
  27.5 2.0 pad_maximum_fusion.1
  29.5 87.6 %shard_map.82 = bf16[8,2,2,816,128]{4,3,2,1,0:T(8,128)(2,1)} custom-call(bf16[4,2,2,816,128]{4,3,2,1,0:T(8,128)(2,1)} %bitcast.64), custom_call_target="tpu_custom_call" | custom-call | bytes 133693440 | tf_op jit(solution)/shard_map/pallas_call | solution.py:190
  119.1 16.6 %shard_map.83 = (f32[16,2,128,128]{3,2,1,0:T(8,128)S(1)}, f32[16,128,128]{2,1,0:T(8,128)}, bf16[16,128,256]{2,1,0:T(8,128)(2,1)}, bf16[24,128,128]{2,1,0:T(8,128)(2,1)}) custom-call(s32[64]{0:T(128)} %get-tuple-element.68.slots, s32[64]{0:T(128)} %compare_convert_fusion.held, s32[64]{0:T(128)} %get-tuple-element.67.partner, s32[17]{0:T(128)} %pad_add_fusion.self_info, ...), custom_call_target="tpu_custom_call" | custom-call | tf_op jit(solution)/shard_map/pallas_call | solution.py:264
  135.8 1.4 slice.60
  140.7 135.8 %shard_map.84 = (bf16[8,2,4,256,256]{4,3,2,1,0:T(8,128)(2,1)}, bf16[4,2,4,256,256]{4,3,2,1,0:T(8,128)(2,1)}, bf16[2,12,128,128]{3,2,1,0:T(8,128)(2,1)}) custom-call(bf16[2,4,256,256]{3,2,1,0:T(8,128)(2,1)} %bitcast.75, bf16[2,12,128,128]{3,2,1,0:T(8,128)(2,1)} %bitcast.78), custom_call_target="tpu_custom_call" | custom-call | bytes 267386880 | tf_op jit(solution)/shard_map/pallas_call | solution.py:190
  276.5 3.0 conditional.1
  276.7 0.7 gather_fusion
  277.6 1.9 gather_fusion.1
  279.6 0.8 fusion.21
  280.5 1.8 subtract_convert_fusion
  282.3 1.9 slice.76
  284.2 2.1 copy.45
  286.3 1.3 broadcast_multiply_fusion
  287.6 0.9 copy.69
  288.5 9.9 %shard_map.85.w_ref = bf16[2048,1024]{1,0:T(8,128)(2,1)} custom-call(s32[32]{0:T(128)} %reshape.163.kept, bf16[1,4,16,128,256]{4,3,2,1,0:T(8,128)(2,1)} %bitcast.70, bf16[2,512,512]{2,1,0:T(8,128)(2,1)} %get-tuple-element.60.hi_ref, bf16[2,512,512]{2,1,0:T(8,128)(2,1)} %get-tuple-element.59.lo_ref, bf16[512,512]{1,0:T(8,128)(2,1)} %bitcast.67), custom_call_target="tpu_custom_call" | custom-call | tf_op jit(solution)/shard_map/pallas_call | solution.py:345
  298.4 14.1 %shard_map.86.v_ref = bf16[1024,4096]{1,0:T(8,128)(2,1)} custom-call(s32[64]{0:T(128)} %reshape.175.kept, bf16[2,4,16,128,256]{4,3,2,1,0:T(8,128)(2,1)} %bitcast.66, bf16[2,512,512]{2,1,0:T(8,128)(2,1)} %get-tuple-element.60.hi_ref, bf16[2,512,512]{2,1,0:T(8,128)(2,1)} %get-tuple-element.59.lo_ref, bf16[512,512]{1,0:T(8,128)(2,1)} %bitcast.68), custom_call_target="tpu_custom_call" | custom-call | tf_op jit(solution)/shard_map/pallas_call | solution.py:345
  312.6 37.2 %shard_map.87 = f32[2048,32,128]{2,1,0:T(8,128)} custom-call(s32[64]{0:T(128)} %get-tuple-element.68.slots, s32[64]{0:T(128)} %compare_convert_fusion.held, s32[17]{0:T(128)} %pad_add_fusion.self_info, f32[2048,32,128]{2,1,0:T(8,128)} %bitcast.60, bf16[2048,1024]{1,0:T(8,128)(2,1)} %shard_map.85.w_ref, bf16[1024,4096]{1,0:T(8,128)(2,1)} %shard_map.86.v_ref, ...), custom_call_target="tpu_custom_call" | custom-call | tf_op jit(solution)/shard_map/pallas_call | solution.py:401
  (71 shorter events, 7.3 us)
Async XLA Ops:
  6.5 275.8 %all-gather.2.cloned.1.call-start = ((), (), s32[]{:S(2)}) async-start(), calls=%async_computation | async-start | bytes 1081344 | tf_op jit(solution)/shard_map/all_gather | solution.py:500
  119.1 18.1 %copy-start.3 = (s32[2,128]{1,0:T(2,128)S(1)}, s32[2,128]{1,0:T(2,128)}, u32[]{:S(2)}) copy-start(s32[2,128]{1,0:T(2,128)} %param.17) | copy-start | bytes 3076
  119.1 18.1 %copy-start = (f32[2,512]{1,0:T(2,128)S(1)}, f32[2,512]{1,0:T(2,128)}, u32[]{:S(2)}) copy-start(f32[2,512]{1,0:T(2,128)} %param.16) | copy-start | bytes 12292
  119.1 18.1 %copy-start.1 = (s32[2,512]{1,0:T(2,128)S(1)}, s32[2,512]{1,0:T(2,128)}, u32[]{:S(2)}) copy-start(s32[2,512]{1,0:T(2,128)} %param.14) | copy-start | bytes 12292
  119.1 18.2 %copy-start.2 = (f32[2,512]{1,0:T(2,128)S(1)}, f32[2,512]{1,0:T(2,128)}, u32[]{:S(2)}) copy-start(f32[2,512]{1,0:T(2,128)} %param.15) | copy-start | bytes 12292
  276.5 3.1 copy-start.4
Sparse Core Ops, SparseCore 0:
  137.3 85.0 all-gather.1

commit v3 on v2

--- a/solution.py
+++ b/solution.py
@@ -104,6 +104,25 @@
     def turn_kept():
         return pltpu.make_async_copy(y_ref.at[h], t_ref.at[h], turn_recv.at[0])
 
+    def ring(way, part, step, behind):
+        origin = row_at(pos - step - behind) if way == 0 else row_at(pos + step + behind)
+        return pltpu.make_async_remote_copy(
+            src_ref=g_ref.at[origin, way, part], dst_ref=g_ref.at[origin, way, part],
+            send_sem=ring_send.at[way, part, step], recv_sem=ring_recv.at[way, part, step],
+            device_id=beside[way], device_id_type=MESH,
+        )
+
+    for way, part in pieces:
+
+        @pl.when(stays)
+        def _():
+            keep(way, part).wait()
+
+        @pl.when(jnp.logical_not(stays))
+        def _():
+            swap(way, part, r).wait_recv()
+
+        ring(way, part, 0, 0).start()
     if keep_row:
         own = pltpu.make_async_copy(x_ref, l_ref.at[c], row_recv.at[0])
         own.start()
@@ -120,25 +139,6 @@
         def _():
             turn(0, h).start()
 
-    def ring(way, part, step, behind):
-        origin = row_at(pos - step - behind) if way == 0 else row_at(pos + step + behind)
-        return pltpu.make_async_remote_copy(
-            src_ref=g_ref.at[origin, way, part], dst_ref=g_ref.at[origin, way, part],
-            send_sem=ring_send.at[way, part, step], recv_sem=ring_recv.at[way, part, step],
-            device_id=beside[way], device_id_type=MESH,
-        )
-
-    for way, part in pieces:
-
-        @pl.when(stays)
-        def _():
-            keep(way, part).wait()
-
-        @pl.when(jnp.logical_not(stays))
-        def _():
-            swap(way, part, r).wait_recv()
-
-        ring(way, part, 0, 0).start()
     for step in range(1, rows - 1):
         for way, part in pieces:
             ring(way, part, step - 1, 1).wait_recv()
@@ -201,7 +201,10 @@
 def face_kernel(slots, held, partner, self_info, place, own_ref, p0, p1, p2, p3, a_ref, c_ref, s_ref, v_ref, t_ref, acc):
     e = pl.program_id(0)
     panel_slots = acc.shape[1] // NB
-    acc[...] = a_ref[0]
+    near = a_ref.shape[1]
+    flat = a_ref.reshape(NB * near, NB)
+    for j in range(panel_slots):
+        acc[:, j * NB : (j + 1) * NB] = flat[pl.ds(j, NB, stride=near), :]
     contract = (((0,), (0,)), ((), ()))
 
     def left(f):
@@ -253,14 +256,14 @@
     v_ref[0] = acc[...].astype(BF16)
 
 
-def faces(traces, partners, base, slots, held, partner, self_info, place, room):
-    row_blocks, width = base.shape[0], base.shape[2]
+def faces(traces, partners, front, width, slots, held, partner, self_info, place, room):
+    row_blocks = traces.shape[0]
     in_specs = [pl.BlockSpec((1, 4, 3, NB, NB), lambda e, *_: (e, 0, 0, 0, 0))]
     for f in range(4):
         in_specs.append(
             pl.BlockSpec((1, 3, NB, NB), lambda e, s, h, p, i, t, f=f: (p[e * 4 + f], 0, 0, 0))
         )
-    in_specs.append(pl.BlockSpec((1, NB, width), lambda e, *_: (e, 0, 0)))
+    in_specs.append(pl.BlockSpec((NB, 8, NB), lambda e, *_: (e, 0, 0)))
     return pl.pallas_call(
         face_kernel,
         grid_spec=pltpu.PrefetchScalarGridSpec(
@@ -282,15 +285,22 @@
             jax.ShapeDtypeStruct((room, NB, NB), BF16),
         ],
         compiler_params=pltpu.CompilerParams(vmem_limit_bytes=VMEM_LIMIT),
-    )(slots, held, partner, self_info, place, traces, partners, partners, partners, partners, base)
-
-
-def panel_kernel(cols, transposed, kept, raw_ref, hi_ref, lo_ref, pivot_ref, out_ref):
+    )(slots, held, partner, self_info, place, traces, partners, partners, partners, partners, front)
+
+
+def panel_kernel(cols, transposed, kept, pivot_kept, raw_ref, hi_ref, lo_ref, every_ref, out_ref, pivot_ref):
     q, t = pl.program_id(0), pl.program_id(1)
     per = raw_ref.shape[2]
     blocks = pl.num_programs(1) * per
     first = q * blocks + t * per
     count = pl.num_programs(0) * blocks
+
+    @pl.when(jnp.logical_and(q == 0, t == 0))
+    def _():
+        for i in range(PB):
+            block = jnp.concatenate([every_ref[i, b] for b in range(PB)], axis=1)
+            block = jnp.where(pivot_kept[i] == 1, block, jnp.zeros_like(block))
+            pivot_ref[:, i * NB : (i + 1) * NB] = block.T
 
     def masked(k, parts):
         return jnp.concatenate(
@@ -330,7 +340,7 @@
         out_ref[:, PW:] = scaled(1, v1)
 
 
-def panels(raw, kept, hi, lo, pivot_rows, transposed):
+def panels(raw, kept, pivot_kept, hi, lo, every, transposed):
     groups, cols, row_blocks, _, width = raw.shape
     per = 4
     steps = row_blocks // per
@@ -345,19 +355,20 @@
     return pl.pallas_call(
         functools.partial(panel_kernel, cols, transposed),
         grid_spec=pltpu.PrefetchScalarGridSpec(
-            num_scalar_prefetch=1,
+            num_scalar_prefetch=2,
             grid=(groups, steps),
             in_specs=[
                 pl.BlockSpec((1, cols, per, NB, width), lambda q, t, *_: (q, 0, t, 0, 0)),
                 whole(hi.shape),
                 whole(lo.shape),
-                whole(pivot_rows.shape),
+                pl.BlockSpec((PB, cols, NB, NB), lambda q, t, *_: (1, 0, 0, 0)),
             ],
             out_specs=out_spec,
+            scratch_shapes=[pltpu.VMEM((PW, PW), BF16)],
         ),
         out_shape=jax.ShapeDtypeStruct(shape, BF16),
         compiler_params=pltpu.CompilerParams(vmem_limit_bytes=VMEM_LIMIT),
-    )(kept, raw, hi, lo, pivot_rows)
+    )(kept, pivot_kept, raw, hi, lo, every)
 
 
 def update_kernel(groups, per, slots, held, self_info, a_ref, w_ref, v_ref, c_ref, d_ref, s_ref, o_ref):
@@ -492,9 +503,9 @@
     here_even = here[:, 0::2].reshape(-1)
     place = jnp.where(here_even & (my_rank < cap), my_even % rows // cols * cap + my_rank, -1)
 
-    base = front_base[:, 0, :, :panel_slots, 0, :].reshape(row_blocks, NB, width)
+    front = front_base.reshape(row_blocks * NB, col_blocks, NB)
     even, self_terms, raw, outgoing = faces(
-        own, partners, base, slots, held, partner, self_info, place, groups * cap
+        own, partners, front, width, slots, held, partner, self_info, place, groups * cap
     )
 
     every = lax.all_gather(raw[0, :, :NB], ("row", "col"), axis=0, tiled=False)
@@ -535,15 +546,13 @@
     by_col = kept.reshape(PANELS, row_blocks, groups, cols)
     col_kept = lax.dynamic_index_in_dim(by_col, c, 3, keepdims=False).transpose(0, 2, 1)
 
-    pivot = every.reshape(rows, cols, NB, NB)[PB : 2 * PB, :PB]
-    pivot = pivot * kept[0, PB : 2 * PB].astype(BF16)[:, None, None, None]
-    pivot_rows = pivot.transpose(1, 3, 0, 2).reshape(PW, PW)
+    every = every.reshape(rows, cols, NB, NB)
+    pivot_kept = kept[0, PB : 2 * PB]
     hi, lo = inverse_matrix(pivot_order, pivot_kind, inverse_diagonal, inverse_coupling)
     shape = (cols, row_blocks, NB, width)
-    w = panels(row_raw.reshape((1,) + shape), row_kept.reshape(-1), hi, lo, pivot_rows, False)
-    v = panels(column_raw.reshape((groups,) + shape), col_kept.reshape(-1), hi, lo, pivot_rows, True)
-
-    front = front_base.reshape(row_blocks * NB, col_blocks, NB)
+    w = panels(row_raw.reshape((1,) + shape), row_kept.reshape(-1), pivot_kept, hi, lo, every, False)
+    v = panels(column_raw.reshape((groups,) + shape), col_kept.reshape(-1), pivot_kept, hi, lo, every, True)
+
     out = update(front, w, v, even, odd, self_terms, slots, held, self_info, groups)
     return out.reshape(front_base.shape)
 

time: 358 us -> 341 us (0.953)
  local copies, waits for them, and re-layouts: 30.9 us -> 13.5 us
    slice x3 -> x0, local copies, waits for them, and re-layouts: 13.6 us -> none  [the longest x1 9.58 us: local(): front_base[:, 0, :, :panel_slots, 0, :].reshape(row_blocks, NB, width)]
    another operation x2 -> x1, local copies, waits for them, and re-layouts: 4.04 us -> 0.07 us  [the longest x1 3.97 us: local(): front_base[:, 0, :, :panel_slots, 0, :].reshape(row_blocks, NB, width)]
  transfers between devices with their start and end apart: 1 -> 1, of which waited for: 0 -> 0; matrix products, arithmetic and copies ran while one was open for 2% -> 3% of each run, Pallas kernels for 38% -> 40%
where the time goes in v3:
time: 341 us
  Pallas kernels  303 us (89%)
  between operations  14.3 us (4%)
  local copies, waits for them, and re-layouts  13.5 us (4%)
  other arithmetic  8.84 us (3%)
    pallas_call x2, Pallas kernels, gather(): pl.pallas_call(functools.partial(gather_kernel, rows, cols, parts, split,...  223 us
    pallas_call x1, Pallas kernels, update(): pl.pallas_call(functools.partial(update_kernel, groups, per), grid_spec=p...  37.1 us
    pallas_call x2, Pallas kernels, panels(): pl.pallas_call(functools.partial(panel_kernel, cols, transposed), grid_sp...  24.5 us
    pallas_call x1, Pallas kernels, faces(): pl.pallas_call(face_kernel, grid_spec=pltpu.PrefetchScalarGridSpec(num_sc...  18 us
  transfers between devices with their start and end apart: 1, of which 0 were waited for; matrix products, arithmetic and copies ran while one was open for 3% of the time, Pallas kernels for 40%

profile of v3, /device:TPU:0, one launch (start us, length us, event | category | flops | bytes accessed | tf_op | source)
XLA Modules:
  0.0 340.6 jit_solution(18026746048532838690)
XLA Ops:
  6.6 0.8 reshape.157
  7.4 0.8 copy.38
  9.0 0.9 slice_bitcast_fusion
  9.9 2.1 slice.45
  12.4 0.7 fusion.51
  14.0 2.0 pad_maximum_fusion.1
  16.0 87.6 %shard_map.82 = bf16[8,2,2,816,128]{4,3,2,1,0:T(8,128)(2,1)} custom-call(bf16[4,2,2,816,128]{4,3,2,1,0:T(8,128)(2,1)} %bitcast.58), custom_call_target="tpu_custom_call" | custom-call | bytes 133693440 | tf_op jit(solution)/shard_map/pallas_call | solution.py:190
  103.7 0.6 pad_add_fusion.self_info
  105.7 18.0 %shard_map.83 = (f32[16,2,128,128]{3,2,1,0:T(8,128)S(1)}, f32[16,128,128]{2,1,0:T(8,128)}, bf16[16,128,256]{2,1,0:T(8,128)(2,1)}, bf16[24,128,128]{2,1,0:T(8,128)(2,1)}) custom-call(s32[64]{0:T(128)} %get-tuple-element.69.slots, s32[64]{0:T(128)} %compare_convert_fusion.held, s32[64]{0:T(128)} %get-tuple-element.68.partner, s32[17]{0:T(128)} %pad_add_fusion.self_info, ...), custom_call_target="tpu_custom_call" | custom-call | tf_op jit(solution)/shard_map/pallas_call | solution.py:267
  123.7 1.4 slice.50
  125.8 0.7 fusion.48
  126.9 0.6 reshape.155.kept
  127.9 0.7 reshape.167.kept
  128.6 0.7 compare_reduce_fusion
  130.0 135.5 %shard_map.84 = (bf16[8,2,4,256,256]{4,3,2,1,0:T(8,128)(2,1)}, bf16[4,2,4,256,256]{4,3,2,1,0:T(8,128)(2,1)}, bf16[2,12,128,128]{3,2,1,0:T(8,128)(2,1)}) custom-call(bf16[2,4,256,256]{3,2,1,0:T(8,128)(2,1)} %bitcast.67, bf16[2,12,128,128]{3,2,1,0:T(8,128)(2,1)} %bitcast.70), custom_call_target="tpu_custom_call" | custom-call | bytes 267386880 | tf_op jit(solution)/shard_map/pallas_call | solution.py:190
  265.6 3.2 conditional.1
  265.8 0.7 gather_fusion
  266.7 1.9 gather_fusion.1
  268.7 0.6 slice_bitcast_fusion.1.pivot_kept
  269.4 0.8 fusion.21
  270.3 1.8 subtract_convert_fusion
  272.1 10.1 %shard_map.85.w_ref = bf16[2048,1024]{1,0:T(8,128)(2,1)} custom-call(s32[32]{0:T(128)} %reshape.155.kept, s32[4]{0:T(128)} %slice_bitcast_fusion.1.pivot_kept, bf16[1,4,16,128,256]{4,3,2,1,0:T(8,128)(2,1)} %bitcast.62, bf16[2,512,512]{2,1,0:T(8,128)(2,1)} %get-tuple-element.60.hi_ref, bf16[2,512,512]{2,1,0:T(8,128)(2,1)} %get-tuple-element.59.lo_ref, ...), custom_call_target="tpu_custom_call" | custom-call | tf_op jit(solution)/shard_map/pallas_call | solution.py:355
  282.2 14.4 %shard_map.86.v_ref = bf16[1024,4096]{1,0:T(8,128)(2,1)} custom-call(s32[64]{0:T(128)} %reshape.167.kept, s32[4]{0:T(128)} %slice_bitcast_fusion.1.pivot_kept, bf16[2,4,16,128,256]{4,3,2,1,0:T(8,128)(2,1)} %bitcast.60, bf16[2,512,512]{2,1,0:T(8,128)(2,1)} %get-tuple-element.60.hi_ref, bf16[2,512,512]{2,1,0:T(8,128)(2,1)} %get-tuple-element.59.lo_ref, ...), custom_call_target="tpu_custom_call" | custom-call | tf_op jit(solution)/shard_map/pallas_call | solution.py:355
  296.6 37.1 %shard_map.87 = f32[2048,32,128]{2,1,0:T(8,128)} custom-call(s32[64]{0:T(128)} %get-tuple-element.69.slots, s32[64]{0:T(128)} %compare_convert_fusion.held, s32[17]{0:T(128)} %pad_add_fusion.self_info, f32[2048,32,128]{2,1,0:T(8,128)} %bitcast.54, bf16[2048,1024]{1,0:T(8,128)(2,1)} %shard_map.85.w_ref, bf16[1024,4096]{1,0:T(8,128)(2,1)} %shard_map.86.v_ref, ...), custom_call_target="tpu_custom_call" | custom-call | tf_op jit(solution)/shard_map/pallas_call | solution.py:412
  (66 shorter events, 5.3 us)
Async XLA Ops:
  6.5 265.5 %all-gather.2.cloned.1.call-start = ((), (), s32[]{:S(2)}) async-start(), calls=%async_computation | async-start | bytes 1081344 | tf_op jit(solution)/shard_map/all_gather | solution.py:511
  105.7 19.5 %copy-start = (f32[2,512]{1,0:T(2,128)S(1)}, f32[2,512]{1,0:T(2,128)}, u32[]{:S(2)}) copy-start(f32[2,512]{1,0:T(2,128)} %param.16) | copy-start | bytes 12292
  105.7 19.5 %copy-start.1 = (s32[2,512]{1,0:T(2,128)S(1)}, s32[2,512]{1,0:T(2,128)}, u32[]{:S(2)}) copy-start(s32[2,512]{1,0:T(2,128)} %param.14) | copy-start | bytes 12292
  105.7 19.5 %copy-start.2 = (f32[2,512]{1,0:T(2,128)S(1)}, f32[2,512]{1,0:T(2,128)}, u32[]{:S(2)}) copy-start(f32[2,512]{1,0:T(2,128)} %param.15) | copy-start | bytes 12292
  105.7 20.1 %copy-start.3 = (s32[2,128]{1,0:T(2,128)S(1)}, s32[2,128]{1,0:T(2,128)}, u32[]{:S(2)}) copy-start(s32[2,128]{1,0:T(2,128)} %param.17) | copy-start | bytes 3076
  265.6 3.8 %copy-start.4 = (s32[2,512]{1,0:T(2,128)S(1)}, s32[2,512]{1,0:T(2,128)}, u32[]{:S(2)}) copy-start(s32[2,512]{1,0:T(2,128)} %param.13) | copy-start | bytes 12292
Sparse Core Ops, SparseCore 0:
  125.2 82.3 all-gather.1
